TPU v7x, 32 devices: a whole 2x2x4 slice. The times are simulated.
32 devices in a mesh: shard: 4 (over y, x), example: 8 (over z, core).
Axes of the slice: x: 2, y: 2, z: 4, core: 2. Of those that a mesh axis runs over, the one named last changes fastest.
Arguments:
- activations: bfloat16 [768, 128, 4096], P('example', None, 'shard'), may hold values from -6 to 6
- out_grads: bfloat16 [768, 128, 4096], P('example', None, 'shard'), may hold values from -6 to 6
- lengths: int32 [768], P('example'), may hold values from 1 to 128
- proj_in: bfloat16 [128, 4096], P(None, 'shard'), may hold values from -0.09375 to 0.09375
- proj_out: bfloat16 [64, 4096], P(None, 'shard'), may hold values from -0.09375 to 0.09375
Outputs:
- ntk_kernel: float32 [768, 768], P('example', 'shard')
All inputs are finite; a program needn't handle non-finite values.
Results may differ from a plain program's by a relative error of at most 0.0014.
Values may be sent and summed in bfloat16 or wider, within the bound.
A program may use at most 128 MiB of HBM per device.

v0:
```python
import math

import jax
import jax.numpy as jnp
import numpy as np
from jax import lax
from jax.sharding import PartitionSpec as P


def pair_tables(n_example):
    pair_list = [(i, j) for i in range(n_example) for j in range(i, n_example)]
    per_device = -(-len(pair_list) // n_example)
    pair_table = np.zeros((n_example, per_device, 2), np.int32)
    where_table = np.zeros((n_example, n_example), np.int32)
    for number, pair_now in enumerate(pair_list):
        device_num = number % n_example
        slot_num = number // n_example
        pair_table[device_num, slot_num, 0] = pair_now[0]
        pair_table[device_num, slot_num, 1] = pair_now[1]
        where_table[pair_now[0], pair_now[1]] = device_num * per_device + slot_num
        where_table[pair_now[1], pair_now[0]] = device_num * per_device + slot_num
    return (pair_table, where_table)


def local(activations, out_grads, lengths, proj_in, proj_out):
    n_shard = lax.axis_size("shard")
    n_example = lax.axis_size("example")
    block_rows = activations.shape[0]
    seq_len = activations.shape[1]
    rows_out = proj_out.shape[0]
    cols_in = proj_in.shape[0]
    per_shard = rows_out // n_shard
    scale_sketch = 1.0 / math.sqrt(seq_len)
    positions = lax.broadcasted_iota(jnp.int32, (block_rows, seq_len), 1)
    token_mask = (positions < lengths[:, None]).astype(jnp.float32)
    left_proj = (
        jnp.einsum("btd,od->bto", out_grads, proj_out, preferred_element_type=jnp.float32)
        * token_mask[:, :, None]
    )
    right_proj = jnp.einsum("btd,id->bti", activations, proj_in, preferred_element_type=jnp.float32)
    left_part, right_part = (
        lax.psum_scatter(left_proj, "shard", scatter_dimension=0, tiled=True),
        lax.psum_scatter(right_proj, "shard", scatter_dimension=0, tiled=True),
    )
    whole_sketch = jnp.einsum(
        "bto,bti->boi",
        left_part,
        right_part,
        precision=lax.Precision.HIGHEST,
        preferred_element_type=jnp.float32,
    )
    whole_sketch = (whole_sketch * scale_sketch).astype(jnp.bfloat16)
    sketch = lax.all_to_all(whole_sketch, "shard", split_axis=1, concat_axis=0, tiled=True)
    sketch = sketch.reshape(block_rows, per_shard * cols_in)
    gathered = lax.all_gather(sketch, "example", axis=0, tiled=True)
    scale_kernel = 1.0 / (rows_out * cols_in)
    blocks = gathered.reshape(n_example, block_rows, per_shard * cols_in)
    pair_table, where_table = pair_tables(n_example)
    my_index = lax.axis_index("example")
    my_pairs = jnp.asarray(pair_table)[my_index]
    row_blocks = blocks[my_pairs[:, 0]]
    col_blocks = blocks[my_pairs[:, 1]]
    tiles = jnp.einsum("kad,kbd->kab", row_blocks, col_blocks, preferred_element_type=jnp.float32)
    tiles = lax.psum(tiles, "shard") * scale_kernel
    every_tile = lax.all_gather(tiles, "example", axis=0, tiled=True)
    col_width = block_rows * n_example // n_shard
    columns = lax.axis_index("shard") * col_width + jnp.arange(col_width, dtype=jnp.int32)
    col_block = columns // block_rows
    inner_col = columns % block_rows
    slot_index = jnp.asarray(where_table)[my_index][col_block]
    flipped = my_index > col_block
    as_stored = every_tile[slot_index, :, inner_col]
    as_mirror = every_tile[slot_index, inner_col, :]
    return jnp.where(flipped[:, None], as_mirror, as_stored).T


def solution(mesh):
    return jax.shard_map(
        local,
        mesh=mesh,
        in_specs=(
            P("example", None, "shard"),
            P("example", None, "shard"),
            P("example"),
            P(None, "shard"),
            P(None, "shard"),
        ),
        out_specs=P("example", "shard"),
        check_vma=False,
    )
```

profile of v0, /device:TPU:0, one launch (start us, length us, event | category | flops | bytes accessed | tf_op | source)
XLA Modules:
  0.0 288.6 jit_solution(6095838720391246799)
XLA Ops:
  6.5 0.0 copy-start
  6.5 0.0 reduce-scatter.3.cloned.1.call-start
  6.5 0.8 fusion.4
  7.3 13.7 %broadcast_multiply_fusion = f32[96,128,64]{1,2,0:T(8,128)} fusion(f32[96,128]{1,0:T(8,128)S(1)} %fusion.4, bf16[96,128,1024]{2,1,0:T(8,128)(2,1)} %param.8, bf16[64,1024]{1,0:T(8,128)(2,1)} %param.11), kind=kOutput, calls=%fused_computation.4 | convolution fusion | flops 1611399168 | bytes 28491776 | tf_op jit(solution)/shard_map/btd,od->bto/dot_general | solution.py:37
  21.0 0.0 reduce-scatter.3.cloned.1.call-update
  21.0 0.0 reduce-scatter.5.cloned.1.call-start
  21.1 0.0 copy-done
  21.1 14.5 %fusion.1 = f32[96,128,128]{2,1,0:T(8,128)} fusion(bf16[96,128,1024]{2,1,0:T(8,128)(2,1)} %param.7, bf16[128,1024]{1,0:T(8,128)(2,1)S(1)} %copy-done), kind=kOutput, calls=%fused_computation.8 | convolution fusion | flops 3221225472 | bytes 31719424 | tf_op jit(solution)/shard_map/btd,id->bti/dot_general | solution.py:40
  35.6 0.0 reduce-scatter.5.cloned.1.call-update
  35.6 0.0 all-gather.3.cloned.1.call-start
  35.6 32.2 %reduce-scatter.3.cloned.1.call-done = f32[24,128,64]{1,2,0:T(8,128)} async-done(((f32[96,128,64]{1,2,0:T(8,128)}), f32[24,128,64]{1,2,0:T(8,128)}) %reduce-scatter.3.cloned.1.call-update) | async-done | bytes 786448 | tf_op jit(solution)/shard_map/reduce_scatter | solution.py:42
  67.8 73.2 %reduce-scatter.5.cloned.1.call-done = f32[24,128,128]{2,1,0:T(8,128)} async-done(((f32[96,128,128]{2,1,0:T(8,128)}), f32[24,128,128]{2,1,0:T(8,128)}) %reduce-scatter.5.cloned.1.call-update) | async-done | bytes 1572880 | tf_op jit(solution)/shard_map/reduce_scatter | solution.py:43
  141.1 3.2 %fusion = bf16[24,64,128]{2,1,0:T(8,128)(2,1)S(1)} fusion(f32[24,128,64]{1,2,0:T(8,128)} %reduce-scatter.3.cloned.1.call-done, f32[24,128,128]{2,1,0:T(8,128)} %reduce-scatter.5.cloned.1.call-done), kind=kOutput, calls=%fused_computation.6 | convolution fusion | flops 302383104 | bytes 2752512 | tf_op jit(solution)/shard_map/bto,bti->boi/dot_general | solution.py:45
  144.2 0.3 copy.13
  144.5 9.8 %all_to_all.15 = bf16[24,64,128]{2,0,1:T(8,128)(2,1)S(1)} all-to-all(bf16[24,64,128]{2,0,1:T(8,128)(2,1)S(1)} %copy.13), channel_id=1, replica_groups=mesh['shard'=4,'example'=8] {'shard'}, dimensions={1} | all-to-all | bytes 786432 | tf_op jit(solution)/shard_map/all_to_all | solution.py:53
  154.3 0.1 copy.14
  154.3 0.8 copy.19
  155.2 0.0 all-gather.3.cloned.1.call-update
  155.2 0.0 all-reduce.2.cloned.1.call-start
  155.3 0.7 dynamic-slice_bitcast_fusion
  156.0 37.1 %all-gather.3.cloned.1.call-done = bf16[768,2048]{1,0:T(8,128)(2,1)} async-done(((bf16[96,2048]{1,0:T(8,128)(2,1)}), bf16[768,2048]{1,0:T(8,128)(2,1)}) %all-gather.3.cloned.1.call-update) | async-done | bytes 3145744 | tf_op jit(solution)/shard_map/all_gather | solution.py:55
  193.1 2.6 gather_fusion.1
  195.7 4.0 %gather_fusion = bf16[5,96,2048]{2,1,0:T(8,128)(2,1)} fusion(bf16[8,96,2048]{2,1,0:T(8,128)(2,1)} %bitcast.42, s32[1024]{0:T(1024)S(1)} %get-tuple-element.16), kind=kCustom, calls=%fused_computation | custom fusion | bytes 3932180 | tf_op jit(solution)/shard_map/gather | solution.py:61
  199.7 2.9 %fusion.15 = f32[5,96,96]{2,1,0:T(8,128)} fusion(bf16[5,96,2048]{2,1,0:T(8,128)(2,1)} %gather_fusion, bf16[5,96,2048]{2,1,0:T(8,128)(2,1)S(1)} %gather_fusion.1), kind=kOutput, calls=%fused_computation.46 | convolution fusion | flops 188743680 | bytes 4116480 | tf_op jit(solution)/shard_map/kad,kbd->kab/dot_general | solution.py:63
  202.6 0.0 all-reduce.2.cloned.1.call-update
  202.6 0.2 all-gather.5.cloned.1.call-start
  202.8 41.6 %all-reduce.2.cloned.1.call-done = f32[5,96,96]{2,1,0:T(8,128)} async-done(((f32[5,96,96]{2,1,0:T(8,128)}), f32[5,96,96]{2,1,0:T(8,128)}) %all-reduce.2.cloned.1.call-update) | async-done | bytes 184336 | tf_op jit(solution)/shard_map/psum | solution.py:64
  244.4 1.7 broadcast_multiply_fusion.1
  246.1 0.0 all-gather.5.cloned.1.call-update
  246.2 0.7 constant_dynamic-slice_fusion
  246.9 0.7 fusion.14
  247.5 4.3 %compare_select_fusion.3 = s32[192,1]{0,1:T(1,128)S(1)} fusion(s32[]{:T(128)} %bitcast.9, s32[]{:T(128)} %bitcast.10, s32[]{:T(128)} %bitcast.11, s32[]{:T(128)} %bitcast.12, s32[]{:T(128)} %bitcast.13, s32[]{:T(128)} %bitcast.15, s32[]{:T(128)} %bitcast.14, s32[]{:T(128)S(6)} %mul.23), kind=kLoop, calls=%fused_computation.21 | loop fusion | flops 4608 | bytes 800 | tf_op jit(solution)/shard_map/gather | solution.py:70
  251.8 0.7 broadcast_select_fusion
  252.5 21.9 %all-gather.5.cloned.1.call-done = f32[40,96,96]{2,1,0:T(8,128)} async-done(((f32[5,96,96]{2,1,0:T(8,128)}), f32[40,96,96]{2,1,0:T(8,128)}) %all-gather.5.cloned.1.call-update) | async-done | bytes 1474576 | tf_op jit(solution)/shard_map/all_gather | solution.py:65
  274.4 0.0 copy-start.1
  274.4 1.9 copy.15
  276.3 2.2 gather_fusion.3
  278.5 2.7 gather_fusion.2
  281.2 0.1 select_bitcast_fusion
  281.3 0.7 copy.16
  282.0 0.0 copy-done.1
  (5 shorter events, 0.1 us)
Async XLA Ops:
  6.5 14.6 %copy-start = (bf16[128,1024]{1,0:T(8,128)(2,1)S(1)}, bf16[128,1024]{1,0:T(8,128)(2,1)}, u32[]{:S(2)}) copy-start(bf16[128,1024]{1,0:T(8,128)(2,1)} %param.10) | copy-start | bytes 786436
  6.5 61.3 %reduce-scatter.3.cloned.1.call-start = ((), (), s32[]{:S(2)}) async-start(), calls=%async_computation.3 | async-start | bytes 3932160 | tf_op jit(solution)/shard_map/reduce_scatter | solution.py:42
  21.0 120.0 %reduce-scatter.5.cloned.1.call-start = ((), (), s32[]{:S(2)}) async-start(), calls=%async_computation.4 | async-start | bytes 7864320 | tf_op jit(solution)/shard_map/reduce_scatter | solution.py:43
  35.6 157.5 %all-gather.3.cloned.1.call-start = ((), (), s32[]{:S(2)}) async-start(), calls=%async_computation.5 | async-start | bytes 3538944 | tf_op jit(solution)/shard_map/all_gather | solution.py:55
  155.2 89.2 %all-reduce.2.cloned.1.call-start = ((), (), s32[]{:S(2)}) async-start(), calls=%async_computation.6 | async-start | bytes 491520 | tf_op jit(solution)/shard_map/psum | solution.py:64
  202.6 71.8 %all-gather.5.cloned.1.call-start = ((), (), s32[]{:S(2)}) async-start(), calls=%async_computation.7 | async-start | bytes 2211840 | tf_op jit(solution)/shard_map/all_gather | solution.py:65
  274.4 7.6 %copy-start.1 = (bf16[128,1024]{1,0:T(8,128)(2,1)S(1)}, bf16[128,1024]{1,0:T(8,128)(2,1)}, u32[]{:S(2)}) copy-start(bf16[128,1024]{1,0:T(8,128)(2,1)} %param.10) | copy-start | bytes 786436
Sparse Core Ops, SparseCore 0:
  21.2 46.6 reduce-scatter.2
  70.8 70.2 reduce-scatter.4
  155.3 37.7 all-gather.2
  202.7 41.6 all-reduce.1
  246.2 28.1 all-gather.4
where the time goes:
time: 289 us
  waiting for transfers between devices  206 us (71%)
  matrix products  34.2 us (12%)
  local copies, waits for them, and re-layouts  17.3 us (6%)
  between operations  13.2 us (5%)
  blocking collectives  9.77 us (3%)
  other arithmetic  7.59 us (3%)
    reduce_scatter x1, waiting for transfers between devices, local(): lax.psum_scatter(right_proj, 'shard', scatter_dimension=0, tiled=True)  73.2 us
    psum x1, waiting for transfers between devices, local(): tiles = lax.psum(tiles, 'shard') * scale_kernel  41.6 us
    all_gather x1, waiting for transfers between devices, local(): gathered = lax.all_gather(sketch, 'example', axis=0, tiled=True)  37.1 us
    reduce_scatter x1, waiting for transfers between devices, local(): lax.psum_scatter(left_proj, 'shard', scatter_dimension=0, tiled=True)  32.2 us
    all_gather x1, waiting for transfers between devices, local(): every_tile = lax.all_gather(tiles, 'example', axis=0, tiled=True)  21.9 us
    dot_general x1, matrix products, local(): jnp.einsum('btd,id->bti', activations, proj_in, preferred_element_type=jn...  14.5 us
    dot_general x1, matrix products, local(): jnp.einsum('btd,od->bto', out_grads, proj_out, preferred_element_type=jnp...  13.7 us
    all_to_all x1, blocking collectives, local(): lax.all_to_all(whole_sketch, 'shard', split_axis=1, concat_axis=0, tiled=...  9.77 us
  transfers between devices with their start and end apart: 5, of which 5 were waited for; matrix products, arithmetic and copies ran while one was open for 7% of the time, Pallas kernels for 0%

commit v1 on v0

v1 whole, which is shorter than its diff:
```python
import functools
import math

import jax
import jax.numpy as jnp
from jax import lax
from jax.experimental import pallas as pl
from jax.experimental.pallas import tpu as pltpu
from jax.sharding import PartitionSpec as P

CORES = 2
GROUP = 4
F32 = jnp.float32
BF16 = jnp.bfloat16
NT = (((1,), (1,)), ((), ()))
TN = (((0,), (0,)), ((), ()))


def fused_kernel(
    n_shard, n_example, chunks, seq_len, scale_sketch, scale_kernel,
    len_ref, acts_ref, grads_ref, pin_ref, pout_ref, out_ref,
    wide, g_buf, a_buf, own1, send1, recv1, sk, arr, tall, gath, ksend, krecv,
    in_sem, s1s, s1r, a2s, a2r, zs, zr, bs, br, kss, krs,
):
    S, G, C, T = n_shard, GROUP, chunks, seq_len
    Z = n_example // CORES
    H = G // 2
    rows_out = pout_ref.shape[0]
    per = rows_out // S
    lanes = pin_ref.shape[0]
    block = S * G
    rows_dev = C * block
    me = lax.axis_index("shard")
    ex = lax.axis_index("example")
    z, core = ex // CORES, ex % CORES
    sib = z * CORES + (1 - core)

    def shard_at(k):
        return lax.rem(me + k, S)

    def z_to(k):
        return lax.rem(z + k, Z) * CORES + core

    def z_from(k):
        return lax.rem(z + Z - k, Z)

    def remote(src, dst, ss, rs, shard, example):
        return pltpu.make_async_remote_copy(
            src_ref=src, dst_ref=dst, send_sem=ss, recv_sem=rs,
            device_id=(shard, example), device_id_type=pl.DeviceIdType.MESH,
        )

    def copy1(c, k):
        return remote(send1.at[c, k - 1], recv1.at[c, k - 1], s1s.at[c, k - 1], s1r.at[c, k - 1], shard_at(k), ex)

    def copy2(c, k):
        return remote(sk.at[c, shard_at(k)], arr.at[c, me], a2s.at[c, k - 1], a2r.at[c, k - 1], shard_at(k), ex)

    def rows_of(e, c):
        return pl.ds(pl.multiple_of(e * rows_dev + c * block, 16), block)

    def copyz(c, k):
        here = gath.at[rows_of(ex, c), :]
        return remote(here, here, zs.at[c, k - 1], zr.at[c, k - 1], me, z_to(k))

    def copyb(c, k):
        here = gath.at[rows_of(z_from(k) * CORES + core, c), :]
        return remote(here, here, bs.at[c, k], br.at[c, k], me, sib)

    def copyk(k):
        return remote(ksend.at[k - 1], krecv.at[k - 1], kss.at[k - 1], krs.at[k - 1], shard_at(k), ex)

    def reads(u, slot):
        c, k = u // S, lax.rem(u, S) + 1
        row = pl.multiple_of((c * block + shard_at(k) * G) * T, 128)
        return (
            pltpu.make_async_copy(grads_ref.at[pl.ds(row, G * T), :], g_buf.at[slot], in_sem.at[slot, 0]),
            pltpu.make_async_copy(acts_ref.at[pl.ds(row, G * T), :], a_buf.at[slot], in_sem.at[slot, 1]),
        )

    for r in reads(0, 0):
        r.start()
    for r in reads(1, 1):
        r.start()

    barrier = pltpu.get_barrier_semaphore()
    for k in range(1, S):
        pl.semaphore_signal(barrier, inc=1, device_id=(shard_at(k), ex), device_id_type=pl.DeviceIdType.MESH)
    for k in range(1, Z):
        pl.semaphore_signal(barrier, inc=1, device_id=(me, z_to(k)), device_id_type=pl.DeviceIdType.MESH)
    pl.semaphore_signal(barrier, inc=1, device_id=(me, sib), device_id_type=pl.DeviceIdType.MESH)

    wide[...] = jnp.zeros_like(wide)
    wide[0, 0:rows_out, :] = pout_ref[...]
    wide[1, rows_out : 2 * rows_out, :] = pout_ref[...]
    pl.semaphore_wait(barrier, S + Z - 1)

    def project(slot, put):
        left = lax.dot_general(g_buf[slot, 0 : H * T, :], wide[0], NT, preferred_element_type=F32)
        left += lax.dot_general(g_buf[slot, H * T :, :], wide[1], NT, preferred_element_type=F32)
        right = lax.dot_general(a_buf[slot], pin_ref[...], NT, preferred_element_type=F32)
        put(0, H * T, left)
        put(H * T, (H + G) * T, right)

    def chunk_body(c, carry):
        for kk in range(S):
            u = c * S + kk
            slot = kk % 2
            for r in reads(u, slot):
                r.wait()
            k = kk + 1
            if k < S:
                def put(lo, hi, v, k=k):
                    send1[c, k - 1, lo:hi, :] = v.astype(BF16)
                project(slot, put)
                copy1(c, k).start()
            else:
                def put(lo, hi, v):
                    own1[c, lo:hi, :] = v
                project(slot, put)

            @pl.when(u + 2 < C * S)
            def _():
                for r in reads(u + 2, slot):
                    r.start()
        return carry

    lax.fori_loop(0, C, chunk_body, 0)

    def make_sketch(c):
        for k in range(1, S):
            copy1(c, k).wait_recv()
        token = lax.broadcasted_iota(jnp.int32, (T, lanes), 0)

        def whole(i):
            at = slice(i * T, (i + 1) * T)
            v = own1[c, at, :]
            for k in range(1, S):
                v = v + recv1[c, k - 1, at, :].astype(F32)
            return v

        first = c * block + me * G
        for p in range(H):
            left = whole(p)
            for half in range(2):
                n = p + half * H
                right = whole(H + n)
                right = jnp.where(token < len_ref[first + n], right, 0.0)
                both = lax.dot_general(left, right, TN, precision=lax.Precision.HIGHEST, preferred_element_type=F32)
                mine = (both[half * rows_out : (half + 1) * rows_out, :] * scale_sketch).astype(BF16)
                for j in range(S):
                    sk[c, j, n] = mine[j * per : (j + 1) * per, :]
        for k in range(1, S):
            copy2(c, k).start()
        arr[c, me] = sk[c, me]

    def spread(c):
        for k in range(1, S):
            copy2(c, k).wait_recv()
        tall[...] = arr[c].reshape(block * per, lanes).astype(F32)
        at = rows_of(ex, c)
        for o in range(per):
            gath[at, o * lanes : (o + 1) * lanes] = tall[pl.ds(o, block, stride=per), :].astype(BF16)
        for k in range(1, Z):
            copyz(c, k).start()
        copyb(c, 0).start()

    def pass_on(c):
        for k in range(1, Z):
            copyz(c, k).wait_recv()
            copyb(c, k).start()

    LAG2, LAG3 = 1, 2

    def tail_body(i, carry):
        @pl.when(i < C)
        def _():
            make_sketch(i)

        @pl.when((i >= LAG2) & (i < C + LAG2))
        def _():
            spread(i - LAG2)

        @pl.when(i >= LAG3)
        def _():
            pass_on(i - LAG3)
        return carry

    lax.fori_loop(0, C + LAG3, tail_body, 0)

    def gather_wait(c, carry):
        for k in range(Z):
            copyb(c, k).wait_recv()
        return carry

    lax.fori_loop(0, C, gather_wait, 0)

    cols = gath.shape[0] // S
    mine = gath.at[pl.ds(pl.multiple_of(ex * rows_dev, 16), rows_dev), :]

    def tile(j):
        other = gath[pl.ds(pl.multiple_of(j * cols, 16), cols), :]
        return lax.dot_general(mine[...], other, NT, preferred_element_type=F32)

    for k in range(1, S):
        ksend[k - 1] = tile(shard_at(k))
        copyk(k).start()
    total = tile(me)

    def drain(c, carry):
        for k in range(1, S):
            copy1(c, k).wait_send()
            copy2(c, k).wait_send()
        for k in range(1, Z):
            copyz(c, k).wait_send()
        for k in range(Z):
            copyb(c, k).wait_send()
        return carry

    lax.fori_loop(0, C, drain, 0)
    for k in range(1, S):
        copyk(k).wait()
        total = total + krecv[k - 1]
    out_ref[...] = total * scale_kernel


def fused(activations, out_grads, lengths, proj_in, proj_out):
    S, E = lax.axis_size("shard"), lax.axis_size("example")
    rows, T, depth = activations.shape
    rows_out, cols_in = proj_out.shape[0], proj_in.shape[0]
    per = rows_out // S
    G, C, Z = GROUP, rows // (S * GROUP), E // CORES
    unit = (G + G // 2) * T
    kernel = functools.partial(
        fused_kernel, S, E, C, T, 1.0 / math.sqrt(T), 1.0 / (rows_out * cols_in)
    )
    dma = pltpu.SemaphoreType.DMA
    cols = rows * E // S
    macs = rows * T * depth * (rows_out + cols_in) + rows * rows * E * per * cols_in
    return pl.pallas_call(
        kernel,
        out_shape=jax.ShapeDtypeStruct((rows, cols), F32),
        in_specs=[
            pl.BlockSpec(memory_space=pltpu.SMEM),
            pl.BlockSpec(memory_space=pl.ANY),
            pl.BlockSpec(memory_space=pl.ANY),
            pl.BlockSpec(memory_space=pltpu.VMEM),
            pl.BlockSpec(memory_space=pltpu.VMEM),
        ],
        out_specs=pl.BlockSpec(memory_space=pltpu.VMEM),
        scratch_shapes=[
            pltpu.VMEM((2, 2 * rows_out, depth), BF16),
            pltpu.VMEM((2, G * T, depth), BF16),
            pltpu.VMEM((2, G * T, depth), BF16),
            pltpu.VMEM((C, unit, cols_in), F32),
            pltpu.VMEM((C, S - 1, unit, cols_in), BF16),
            pltpu.VMEM((C, S - 1, unit, cols_in), BF16),
            pltpu.VMEM((C, S, G, per, cols_in), BF16),
            pltpu.VMEM((C, S, G, per, cols_in), BF16),
            pltpu.VMEM((S * G * per, cols_in), F32),
            pltpu.VMEM((E * rows, per * cols_in), BF16),
            pltpu.VMEM((S - 1, rows, cols), F32),
            pltpu.VMEM((S - 1, rows, cols), F32),
            dma((2, 2)),
            dma((C, S - 1)),
            dma((C, S - 1)),
            dma((C, S - 1)),
            dma((C, S - 1)),
            dma((C, Z - 1)),
            dma((C, Z - 1)),
            dma((C, Z)),
            dma((C, Z)),
            dma((S - 1,)),
            dma((S - 1,)),
        ],
        compiler_params=pltpu.CompilerParams(
            collective_id=0, has_side_effects=True, vmem_limit_bytes=48 * 2**20
        ),
        cost_estimate=pl.CostEstimate(
            flops=2 * macs, bytes_accessed=4 * rows * T * depth, transcendentals=0
        ),
    )(
        lengths,
        activations.reshape(rows * T, depth),
        out_grads.reshape(rows * T, depth),
        proj_in,
        proj_out,
    )


def plain(activations, out_grads, lengths, proj_in, proj_out):
    n_shard = lax.axis_size("shard")
    rows, seq_len = activations.shape[:2]
    rows_out, cols_in = proj_out.shape[0], proj_in.shape[0]
    per_shard = rows_out // n_shard
    positions = lax.broadcasted_iota(jnp.int32, (rows, seq_len), 1)
    token_mask = (positions < lengths[:, None]).astype(F32)
    left = jnp.einsum("btd,od->bto", out_grads, proj_out, preferred_element_type=F32)
    left = left * token_mask[:, :, None]
    right = jnp.einsum("btd,id->bti", activations, proj_in, preferred_element_type=F32)
    left = lax.psum_scatter(left, "shard", scatter_dimension=0, tiled=True)
    right = lax.psum_scatter(right, "shard", scatter_dimension=0, tiled=True)
    sketch = jnp.einsum(
        "bto,bti->boi", left, right, precision=lax.Precision.HIGHEST, preferred_element_type=F32
    )
    sketch = (sketch * (1.0 / math.sqrt(seq_len))).astype(BF16)
    sketch = lax.all_to_all(sketch, "shard", split_axis=1, concat_axis=0, tiled=True)
    sketch = sketch.reshape(rows, per_shard * cols_in)
    every = lax.all_gather(sketch, "example", axis=0, tiled=True)
    tiles = jnp.einsum("ad,bd->ab", sketch, every, preferred_element_type=F32)
    tiles = lax.psum_scatter(tiles, "shard", scatter_dimension=1, tiled=True)
    return tiles * (1.0 / (rows_out * cols_in))


def local(activations, out_grads, lengths, proj_in, proj_out):
    S, E = lax.axis_size("shard"), lax.axis_size("example")
    rows, T, depth = activations.shape
    rows_out, cols_in = proj_out.shape[0], proj_in.shape[0]
    fits = (
        S >= 2 and S % 2 == 0 and E % CORES == 0 and E > CORES
        and rows_out % (16 * S) == 0 and 2 * rows_out == cols_in and cols_in % 128 == 0
        and T % 128 == 0 and depth % 128 == 0
        and rows % (S * GROUP) == 0 and (S * GROUP) % 16 == 0 and (rows * E) % (16 * S) == 0
    )
    return (fused if fits else plain)(activations, out_grads, lengths, proj_in, proj_out)


def solution(mesh):
    return jax.shard_map(
        local,
        mesh=mesh,
        in_specs=(
            P("example", None, "shard"),
            P("example", None, "shard"),
            P("example"),
            P(None, "shard"),
            P(None, "shard"),
        ),
        out_specs=P("example", "shard"),
        check_vma=False,
    )
```

time: 289 us -> 107 us (0.37)
  waiting for transfers between devices: 206 us -> 0 us
  Pallas kernels: 0 us -> 103 us
  matrix products: 34.2 us -> 0 us
  local copies, waits for them, and re-layouts: 17.3 us -> 3.15 us
  between operations: 13.2 us -> 0.01 us
  blocking collectives: 9.77 us -> 0 us
  other arithmetic: 7.59 us -> 0 us
    reduce_scatter x2 -> x0, waiting for transfers between devices: 105 us -> none  [the longest x1 73.2 us: local(): lax.psum_scatter(right_proj, 'shard', scatter_dimension=0, tiled=True)]
    pallas_call x0 -> x1, Pallas kernels: none -> 103 us  [fused(): pl.pallas_call(kernel, out_shape=jax.ShapeDtypeStruct((rows, cols), F32),...]
    all_gather x2 -> x0, waiting for transfers between devices: 59 us -> none  [the longest x1 37.1 us: local(): gathered = lax.all_gather(sketch, 'example', axis=0, tiled=True)]
    psum x1 -> x0, waiting for transfers between devices: 41.6 us -> none  [local(): tiles = lax.psum(tiles, 'shard') * scale_kernel]
    dot_general x4 -> x0, matrix products: 34.2 us -> none  [the longest x1 14.5 us: local(): jnp.einsum('btd,id->bti', activations, proj_in, preferred_element_type=jn...]
    gather x5 -> x0, local copies, waits for them, and re-layouts: 12.1 us -> none  [the longest x1 4 us: local(): row_blocks = blocks[my_pairs[:, 0]]]
    all_to_all x1 -> x0, blocking collectives: 9.77 us -> none  [local(): lax.all_to_all(whole_sketch, 'shard', split_axis=1, concat_axis=0, tiled=...]
    gather x4 -> x0, other arithmetic: 5 us -> none  [the longest x3 4.99 us: local(): slot_index = jnp.asarray(where_table)[my_index][col_block]]
  transfers between devices with their start and end apart: 5 -> 0, of which waited for: 5 -> 0; matrix products, arithmetic and copies ran while one was open for 7% -> 0% of each run, Pallas kernels for 0% -> 0%
where the time goes in v1:
time: 107 us
  Pallas kernels  103 us (96%)
  local copies, waits for them, and re-layouts  3.15 us (3%)
    pallas_call x1, Pallas kernels, fused(): pl.pallas_call(kernel, out_shape=jax.ShapeDtypeStruct((rows, cols), F32),...  103 us
    unnamed x7, local copies, waits for them, and re-layouts  3.15 us

profile of v1, /device:TPU:0, one launch (start us, length us, event | category | flops | bytes accessed | tf_op | source)
XLA Modules:
  0.0 106.6 jit_solution(6111269490658031074)
XLA Ops:
  0.0 0.0 copy-start
  0.0 0.9 copy-done
  1.0 0.0 copy-start.1
  1.0 0.9 copy-done.1
  1.9 0.0 copy-start.2
  1.9 0.7 copy-done.2
  2.5 103.4 %shard_map.55 = f32[96,192]{1,0:T(8,128)S(1)} custom-call(s32[96]{0:T(128)S(1)} %copy-done.2, bf16[12288,1024]{1,0:T(8,128)(2,1)} %bitcast.2, bf16[12288,1024]{1,0:T(8,128)(2,1)} %bitcast.3, bf16[128,1024]{1,0:T(8,128)(2,1)S(1)} %copy-done, bf16[64,1024]{1,0:T(8,128)(2,1)S(1)} %copy-done.1), custom_call_target="tpu_custom_call" | custom-call | flops 5133828096 | bytes 50331648 | tf_op jit(solution)/shard_map/pallas_call | solution.py:240
  105.9 0.6 copy.7
Async XLA Ops:
  0.0 0.9 copy-start
  1.0 0.9 copy-start.1
  1.9 0.7 copy-start.2

commit v2 on v1

--- a/solution.py
+++ b/solution.py
@@ -9,9 +9,11 @@
 from jax.sharding import PartitionSpec as P
 
 CORES = 2
+DEPTH = 4
 GROUP = 4
 F32 = jnp.float32
 BF16 = jnp.bfloat16
+NN = (((1,), (0,)), ((), ()))
 NT = (((1,), (1,)), ((), ()))
 TN = (((0,), (0,)), ((), ()))
 
@@ -19,8 +21,8 @@
 def fused_kernel(
     n_shard, n_example, chunks, seq_len, scale_sketch, scale_kernel,
     len_ref, acts_ref, grads_ref, pin_ref, pout_ref, out_ref,
-    wide, g_buf, a_buf, own1, send1, recv1, sk, arr, tall, gath, ksend, krecv,
-    in_sem, s1s, s1r, a2s, a2r, zs, zr, bs, br, kss, krs,
+    pin_v, pout_v, wide, right_w, g_buf, a_buf, own1, send1, recv1, sk, arr, tall, gath, ksend, krecv,
+    w_sem, in_sem, s1s, s1r, a2s, a2r, zs, zr, bs, br, kss, krs,
 ):
     S, G, C, T = n_shard, GROUP, chunks, seq_len
     Z = n_example // CORES
@@ -78,10 +80,15 @@
             pltpu.make_async_copy(acts_ref.at[pl.ds(row, G * T), :], a_buf.at[slot], in_sem.at[slot, 1]),
         )
 
-    for r in reads(0, 0):
-        r.start()
-    for r in reads(1, 1):
-        r.start()
+    weights = (
+        pltpu.make_async_copy(pin_ref, pin_v, w_sem.at[0]),
+        pltpu.make_async_copy(pout_ref, pout_v, w_sem.at[1]),
+    )
+    for w in weights:
+        w.start()
+    for u in range(DEPTH):
+        for r in reads(u, u):
+            r.start()
 
     barrier = pltpu.get_barrier_semaphore()
     for k in range(1, S):
@@ -90,22 +97,26 @@
         pl.semaphore_signal(barrier, inc=1, device_id=(me, z_to(k)), device_id_type=pl.DeviceIdType.MESH)
     pl.semaphore_signal(barrier, inc=1, device_id=(me, sib), device_id_type=pl.DeviceIdType.MESH)
 
-    wide[...] = jnp.zeros_like(wide)
-    wide[0, 0:rows_out, :] = pout_ref[...]
-    wide[1, rows_out : 2 * rows_out, :] = pout_ref[...]
+    for w in weights:
+        w.wait()
+    right_w[...] = pin_v[...].astype(F32).T.astype(BF16)
+    thin = pout_v[...].astype(F32)
+    zero = jnp.zeros_like(thin)
+    wide[0] = jnp.concatenate([thin, zero], axis=0).T.astype(BF16)
+    wide[1] = jnp.concatenate([zero, thin], axis=0).T.astype(BF16)
     pl.semaphore_wait(barrier, S + Z - 1)
 
     def project(slot, put):
-        left = lax.dot_general(g_buf[slot, 0 : H * T, :], wide[0], NT, preferred_element_type=F32)
-        left += lax.dot_general(g_buf[slot, H * T :, :], wide[1], NT, preferred_element_type=F32)
-        right = lax.dot_general(a_buf[slot], pin_ref[...], NT, preferred_element_type=F32)
+        left = lax.dot_general(g_buf[slot, 0 : H * T, :], wide[0], NN, preferred_element_type=F32)
+        left += lax.dot_general(g_buf[slot, H * T :, :], wide[1], NN, preferred_element_type=F32)
+        right = lax.dot_general(a_buf[slot], right_w[...], NN, preferred_element_type=F32)
         put(0, H * T, left)
         put(H * T, (H + G) * T, right)
 
-    def chunk_body(c, carry):
+    def project_chunk(c):
         for kk in range(S):
             u = c * S + kk
-            slot = kk % 2
+            slot = kk % DEPTH
             for r in reads(u, slot):
                 r.wait()
             k = kk + 1
@@ -119,13 +130,10 @@
                     own1[c, lo:hi, :] = v
                 project(slot, put)
 
-            @pl.when(u + 2 < C * S)
+            @pl.when(u + DEPTH < C * S)
             def _():
-                for r in reads(u + 2, slot):
+                for r in reads(u + DEPTH, slot):
                     r.start()
-        return carry
-
-    lax.fori_loop(0, C, chunk_body, 0)
 
     def make_sketch(c):
         for k in range(1, S):
@@ -170,23 +178,16 @@
             copyz(c, k).wait_recv()
             copyb(c, k).start()
 
-    LAG2, LAG3 = 1, 2
-
-    def tail_body(i, carry):
-        @pl.when(i < C)
-        def _():
-            make_sketch(i)
-
-        @pl.when((i >= LAG2) & (i < C + LAG2))
-        def _():
-            spread(i - LAG2)
-
-        @pl.when(i >= LAG3)
-        def _():
-            pass_on(i - LAG3)
+    steps = (project_chunk, make_sketch, spread, pass_on)
+
+    def body(i, carry):
+        for lag, step in enumerate(steps):
+            @pl.when((i >= lag) & (i < C + lag))
+            def _(lag=lag, step=step):
+                step(i - lag)
         return carry
 
-    lax.fori_loop(0, C + LAG3, tail_body, 0)
+    lax.fori_loop(0, C + len(steps) - 1, body, 0)
 
     def gather_wait(c, carry):
         for k in range(Z):
@@ -244,14 +245,17 @@
             pl.BlockSpec(memory_space=pltpu.SMEM),
             pl.BlockSpec(memory_space=pl.ANY),
             pl.BlockSpec(memory_space=pl.ANY),
-            pl.BlockSpec(memory_space=pltpu.VMEM),
-            pl.BlockSpec(memory_space=pltpu.VMEM),
+            pl.BlockSpec(memory_space=pl.ANY),
+            pl.BlockSpec(memory_space=pl.ANY),
         ],
         out_specs=pl.BlockSpec(memory_space=pltpu.VMEM),
         scratch_shapes=[
-            pltpu.VMEM((2, 2 * rows_out, depth), BF16),
-            pltpu.VMEM((2, G * T, depth), BF16),
-            pltpu.VMEM((2, G * T, depth), BF16),
+            pltpu.VMEM((cols_in, depth), BF16),
+            pltpu.VMEM((rows_out, depth), BF16),
+            pltpu.VMEM((2, depth, 2 * rows_out), BF16),
+            pltpu.VMEM((depth, cols_in), BF16),
+            pltpu.VMEM((DEPTH, G * T, depth), BF16),
+            pltpu.VMEM((DEPTH, G * T, depth), BF16),
             pltpu.VMEM((C, unit, cols_in), F32),
             pltpu.VMEM((C, S - 1, unit, cols_in), BF16),
             pltpu.VMEM((C, S - 1, unit, cols_in), BF16),
@@ -261,7 +265,8 @@
             pltpu.VMEM((E * rows, per * cols_in), BF16),
             pltpu.VMEM((S - 1, rows, cols), F32),
             pltpu.VMEM((S - 1, rows, cols), F32),
-            dma((2, 2)),
+            dma((2,)),
+            dma((DEPTH, 2)),
             dma((C, S - 1)),
             dma((C, S - 1)),
             dma((C, S - 1)),

time: 107 us -> 87.2 us (0.81)
  Pallas kernels: 103 us -> 83.9 us
    pallas_call x1, Pallas kernels: 103 us -> 83.9 us  [fused(): pl.pallas_call(kernel, out_shape=jax.ShapeDtypeStruct((rows, cols), F32),...]
where the time goes in v2:
time: 87.2 us; the launch traced here: 87 us
  Pallas kernels  83.9 us (96%)
  local copies, waits for them, and re-layouts  3.15 us (4%)
    pallas_call x1, Pallas kernels, fused(): pl.pallas_call(kernel, out_shape=jax.ShapeDtypeStruct((rows, cols), F32),...  83.9 us
    unnamed x7, local copies, waits for them, and re-layouts  3.15 us

profile of v2, /device:TPU:0, one launch (start us, length us, event | category | flops | bytes accessed | tf_op | source)
XLA Modules:
  0.0 87.0 jit_solution(2020356681323623314)
XLA Ops:
  0.0 0.0 copy-start
  0.0 0.9 %copy-done = bf16[128,1024]{1,0:T(8,128)(2,1)S(1)} copy-done((bf16[128,1024]{1,0:T(8,128)(2,1)S(1)}, bf16[128,1024]{1,0:T(8,128)(2,1)}, u32[]{:S(2)}) %copy-start) | copy-done | bytes 262168
  1.0 0.0 copy-start.1
  1.0 0.9 %copy-done.1 = bf16[64,1024]{1,0:T(8,128)(2,1)S(1)} copy-done((bf16[64,1024]{1,0:T(8,128)(2,1)S(1)}, bf16[64,1024]{1,0:T(8,128)(2,1)}, u32[]{:S(2)}) %copy-start.1) | copy-done | bytes 131096
  1.9 0.0 copy-start.2
  1.9 0.7 copy-done.2
  2.5 83.9 %shard_map.55 = f32[96,192]{1,0:T(8,128)S(1)} custom-call(s32[96]{0:T(128)S(1)} %copy-done.2, bf16[12288,1024]{1,0:T(8,128)(2,1)} %bitcast.2, bf16[12288,1024]{1,0:T(8,128)(2,1)} %bitcast.3, bf16[128,1024]{1,0:T(8,128)(2,1)S(1)} %copy-done, bf16[64,1024]{1,0:T(8,128)(2,1)S(1)} %copy-done.1), custom_call_target="tpu_custom_call" | custom-call | flops 5133828096 | bytes 50331648 | tf_op jit(solution)/shard_map/pallas_call | solution.py:241
  86.4 0.6 copy.7
Async XLA Ops:
  0.0 0.9 %copy-start = (bf16[128,1024]{1,0:T(8,128)(2,1)S(1)}, bf16[128,1024]{1,0:T(8,128)(2,1)}, u32[]{:S(2)}) copy-start(bf16[128,1024]{1,0:T(8,128)(2,1)} %pin_ref.1) | copy-start | bytes 786436
  1.0 0.9 %copy-start.1 = (bf16[64,1024]{1,0:T(8,128)(2,1)S(1)}, bf16[64,1024]{1,0:T(8,128)(2,1)}, u32[]{:S(2)}) copy-start(bf16[64,1024]{1,0:T(8,128)(2,1)} %pout_ref.1) | copy-start | bytes 393220
  1.9 0.7 copy-start.2
